TPU v7x, 128 devices: a whole 4x4x4 slice. The times are simulated.
128 devices in a mesh: group: 8 (over y, core), dev: 16 (over x, z).
Axes of the slice: x: 4, y: 4, z: 4, core: 2. Of those that a mesh axis runs over, the one named last changes fastest.
Arguments:
- rhs: bfloat16 [65536, 512], P(('group', 'dev')), may hold values from -6 to 6
- basis: bfloat16 [65536, 64, 64], P(('group', 'dev')), may hold values from -0.75 to 0.75
- transfer: bfloat16 [65536, 64, 64], P(('group', 'dev')), may hold values from -0.25 to 0.25
- near_blocks: bfloat16 [65536, 2, 64, 64], P(('group', 'dev')), may hold values from -0.5 to 0.5
- near_off: int32 [65536, 2], P(('group', 'dev')), may hold values from 0 to 16
- xch_idx: int32 [65536], P(('group', 'dev')), may hold values from 0 to 511, as said below
- shift_idx: int32 [65536], P(('group', 'dev')), may hold values from 0 to 511, as said below
- leaf_slot: int32 [65536, 2], P(('group', 'dev')), may hold values from 0 to 1023, as said below
- leaf_op: int32 [65536, 2], P(('group', 'dev')), may hold values from 0 to 315
- parent_slot: int32 [8192, 16], P(('group', 'dev')), may hold values from 0 to 1023, as said below
- parent_op: int32 [8192, 16], P(('group', 'dev')), may hold values from 0 to 315
- leaf_ops: bfloat16 [316, 64, 64], replicated, may hold values from -0.5 to 0.5
- parent_ops: bfloat16 [316, 64, 64], replicated, may hold values from -0.1875 to 0.1875
Outputs:
- potential: bfloat16 [65536, 512], P(('group', 'dev'))
Inputs may be any that keep to these rules, and one draw needn't show every extreme that they name: `xch_idx`: each device's 512 entries name each of its local leaves exactly once. `shift_idx`: each device's 512 entries name each of its local leaves exactly once. `leaf_slot`: on each device the 512 x 2 entries name every received slot exactly once. `parent_slot`: on each device the 64 x 16 entries name every parent of its group exactly once.
All inputs are finite; a program needn't handle non-finite values.
Results may differ from a plain program's by a relative error of at most 0.0051.
Values may be sent and summed in bfloat16 or wider, within the bound.
A program may use at most 256 MiB of HBM per device.

v0:
```python
import functools

import jax
import jax.numpy as jnp
from jax import lax
from jax.experimental import pallas as pl
from jax.experimental.pallas import tpu as pltpu
from jax.sharding import PartitionSpec as P

MESH = pl.DeviceIdType.MESH
f32 = jnp.float32
bf16 = jnp.bfloat16
i32 = jnp.int32

LEAVES = 512
RANK = 64
NRHS = 8
ROW = NRHS * RANK
NOPS = 316
REACH = 8
PAR = 64
NDEV = 16
CAPL = 32
CAPG = 256
LANES = 128
TILES = LEAVES // LANES
KB = 8


def lanes(t):
    return pl.ds(pl.multiple_of(t * LANES, LANES), LANES)


def hot(rows, row, first=0):
    at = lax.broadcasted_iota(i32, (rows, row.shape[1]), 0) + first
    return jnp.where(at == row, 1.0, 0.0).astype(bf16)


def dot(a, b, dims=((1,), (0,))):
    return lax.dot_general(a, b, (dims, ((), ())), preferred_element_type=f32)


def upward(mats, vecs, out, before):
    def tile(i, _):
        t, half = i // 2, i % 2
        before(i)
        ks = pl.ds(pl.multiple_of(half * 32, 32), 32)

        def eight(pb, acc):
            for pi in range(8):
                p = pb * 8 + pi
                b = mats[p, ks, lanes(t)].astype(f32).reshape(4, 8, LANES)
                acc = tuple(
                    acc[r] + b * vecs[t, r, pl.ds(p, 8, stride=0), :][None]
                    for r in range(NRHS)
                )
            return acc

        zero = jnp.zeros((4, 8, LANES), f32)
        acc = lax.fori_loop(0, RANK // 8, eight, (zero,) * NRHS)
        for r in range(NRHS):
            out(t, r, ks, acc[r].reshape(32, LANES))
        return 0

    lax.fori_loop(0, 2 * TILES, tile, 0)


def madd(acc, mats, vecs, width, r0, rb):
    for mp in range(4):
        a = mats(pl.ds(mp * 16, 16)).astype(f32)
        for h in range(2):
            c = vecs(pl.ds(r0, rb), pl.ds(mp * 16 + h * 8, 8))
            v = a[None, :, h * 8 : h * 8 + 8] * c[:, None]
            acc = v if acc is None else acc + v
    return acc


def settle(part, out, pos):
    for r in range(NRHS):
        total = None
        for s in range(8):
            v = part[r, pl.ds(s, KB, stride=8), :]
            total = v if total is None else total + v
        out(pos, r, total)


def body(
    basis_h, trans_h, near_h, lops_h, pops_h, rhs_h, xt_ref, idx_ref, out_ref,
    basis, trans, near, lops, pops, xf, lcf, lcb, send, recv, recvt, pbuf, rim, hots,
    gath, nacc, lacc, pacc, e0, e1, part, child, load, tx, rx,
):
    g, me = lax.axis_index("group"), lax.axis_index("dev")
    n_group = lax.axis_size("group")
    right, left = lax.rem(me + 1, NDEV), lax.rem(me + NDEV - 1, NDEV)
    upper, lower = lax.rem(g + 1, n_group), lax.rem(g + n_group - 1, n_group)

    b_loads = [
        pltpu.make_async_copy(basis_h.at[:, :, pl.ds(t * LANES, LANES)], basis.at[:, :, pl.ds(t * LANES, LANES)], load.at[t])
        for t in range(TILES)
    ]
    t_load = pltpu.make_async_copy(trans_h, trans, load.at[4])
    n_loads = [pltpu.make_async_copy(near_h.at[j], near.at[j], load.at[5 + j]) for j in range(2)]
    l_load = pltpu.make_async_copy(lops_h, lops, load.at[7])
    p_load = pltpu.make_async_copy(pops_h, pops, load.at[8])
    for c in (*b_loads, t_load, *n_loads, l_load, p_load):
        c.start()

    barrier = pltpu.get_barrier_semaphore()
    for o in range(1, NDEV):
        pl.semaphore_signal(barrier, inc=1, device_id={"dev": lax.rem(me + o, NDEV)}, device_id_type=MESH)
    for other in (upper, lower):
        pl.semaphore_signal(barrier, inc=1, device_id={"group": other}, device_id_type=MESH)

    for t in range(TILES):
        xf[t] = xt_ref[:, pl.ds(t * LANES, LANES)].astype(f32).reshape(NRHS, RANK, LANES)

    def put_leaf(t, r, ks, v):
        b = v.astype(bf16)
        lcb[r, ks, lanes(t)] = b
        lcf[t, r, ks, :] = b.astype(f32)

    def wait_basis(i):
        for t in range(TILES):

            @pl.when(i == 2 * t)
            def _():
                b_loads[t].wait()

    upward(basis, xf, put_leaf, wait_basis)

    def pick(b, _):
        row = idx_ref[8 + b].astype(f32)
        col = jnp.transpose(jnp.broadcast_to(row, (LANES, LANES)))
        at = lax.broadcasted_iota(i32, (LANES, LANES), 1).astype(f32)
        pieces = [jnp.where(at + float(t * LANES) == col, 1.0, 0.0).astype(bf16) for t in range(TILES)]
        chosen = dot(jnp.concatenate(pieces, axis=1), lcb[...].reshape(ROW, LEAVES), ((1,), (1,)))
        send[pl.ds(pl.multiple_of(b * LANES, LANES), LANES), :] = chosen.astype(bf16)
        return 0

    lax.fori_loop(0, 8, pick, 0)

    pl.semaphore_wait(barrier, NDEV + 1)
    rims = [
        pltpu.make_async_remote_copy(
            src_ref=rhs_h.at[pl.ds(first, 16)], dst_ref=rim.at[s], send_sem=tx.at[32 + s], recv_sem=rx.at[32 + s],
            device_id={"dev": to}, device_id_type=MESH)
        for s, first, to in ((0, LEAVES - 16, right), (1, 0, left))
    ]
    shifts = [
        pltpu.make_async_remote_copy(
            src_ref=send.at[pl.ds(512 + s * CAPG, CAPG)], dst_ref=recv.at[pl.ds(512 + s * CAPG, CAPG)],
            send_sem=tx.at[30 + s], recv_sem=rx.at[30 + s], device_id={"group": to}, device_id_type=MESH)
        for s, to in ((0, upper), (1, lower))
    ]

    def leaf_copy(o):
        to = lax.rem(me + o, NDEV)
        return pltpu.make_async_remote_copy(
            src_ref=send.at[pl.ds(pl.multiple_of(to * CAPL, CAPL), CAPL)],
            dst_ref=recv.at[pl.ds(pl.multiple_of(me * CAPL, CAPL), CAPL)],
            send_sem=tx.at[o - 1], recv_sem=rx.at[o - 1], device_id={"dev": to}, device_id_type=MESH)

    def parent_copy(o):
        to = lax.rem(me + o, NDEV)
        mine = pbuf.at[pl.ds(pl.multiple_of(me * PAR, PAR), PAR)]
        return pltpu.make_async_remote_copy(
            src_ref=mine, dst_ref=mine, send_sem=tx.at[14 + o], recv_sem=rx.at[14 + o],
            device_id={"dev": to}, device_id_type=MESH)

    for c in (*rims, *shifts):
        c.start()
    for o in range(1, NDEV):
        leaf_copy(o).start()
    own = pl.ds(pl.multiple_of(me * CAPL, CAPL), CAPL)
    recv[own, :] = send[own, :]

    t_load.wait()

    def put_parent(t, r, ks, v):
        child[t, r, ks, :] = v

    upward(trans, lcf, put_parent, lambda i: None)
    at = lax.broadcasted_iota(i32, (PAR, LANES), 1) // 8
    q = lax.broadcasted_iota(i32, (PAR, LANES), 0)
    total = None
    for t in range(TILES):
        pool = jnp.where(at + t * 16 == q, 1.0, 0.0).astype(bf16)
        v = child[t].reshape(ROW, LANES)
        high = v.astype(bf16)
        low = (v - high.astype(f32)).astype(bf16)
        s = dot(pool, high, ((1,), (1,))) + dot(pool, low, ((1,), (1,)))
        total = s if total is None else total + s
    pbuf[pl.ds(pl.multiple_of(me * PAR, PAR), PAR), :] = total.astype(bf16)
    for o in range(1, NDEV):
        parent_copy(o).start()

    for c in rims:
        c.wait_recv()
    rim_rows = jnp.concatenate([rim[0], rim[1]], axis=0)
    rim_t = jnp.transpose(rim_rows.astype(f32)).astype(bf16)

    def partners(b, _):
        j, t = b // TILES, lax.rem(b, TILES)
        off = idx_ref[b]
        leaf = lax.broadcasted_iota(i32, (1, LANES), 1) + t * LANES + off - REACH
        leaf = jnp.where((me == 0) & (leaf < 0), -100, leaf)
        leaf = jnp.where((me == NDEV - 1) & (leaf >= LEAVES), -100, leaf)
        at = lax.broadcasted_iota(i32, (32, LANES), 0)
        at = jnp.where(at < 16, at - 16, at + (LEAVES - 16))
        edge = jnp.where(at == leaf, 1.0, 0.0).astype(bf16)
        v = dot(xt_ref[...], hot(LEAVES, leaf)) + dot(rim_t, edge)
        gath[b] = v.reshape(NRHS, RANK, LANES)
        return 0

    lax.fori_loop(0, 8, partners, 0)
    for c in n_loads:
        c.wait()

    def near_step(i, _):
        t, kb = i // 8, lax.rem(i, 8)
        for r0 in (0, 4):
            acc = None
            for j in range(2):
                acc = madd(
                    acc,
                    lambda ms: near[j, pl.ds(pl.multiple_of(kb * KB, KB), KB), ms, lanes(t)],
                    lambda rs, ms: gath[j * TILES + t, rs, ms, :],
                    KB, r0, 4)
            nacc[t, pl.ds(r0, 4), pl.ds(pl.multiple_of(kb * 64, 64), 64), :] = acc.reshape(4, 64, LANES)
        return 0

    lax.fori_loop(0, 32, near_step, 0)

    def turned(src):
        def block(b, _):
            rows = src[pl.ds(pl.multiple_of(b * LANES, LANES), LANES), :]
            recvt[:, lanes(b)] = jnp.transpose(rows.astype(f32)).astype(bf16)
            return 0

        lax.fori_loop(0, 8, block, 0)

    def gather(row_of):
        def block(b, _):
            gath[b] = dot(recvt[...], hot(1024, row_of(b))).reshape(NRHS, RANK, LANES)
            return 0

        lax.fori_loop(0, 8, block, 0)

    def coupling(ops, first, last):
        def spread(i, e_ref):
            i = jnp.minimum(i, 31)
            pair, kb = i // 8, lax.rem(i, 8)
            rows = ops[pl.ds(pl.multiple_of(kb * KB, KB), KB)].reshape(KB * RANK, NOPS)
            e_ref[...] = dot(rows, hots[pair]).reshape(KB, RANK, 2 * LANES)

        def step(i, e_ref):
            pair, kb = i // 8, lax.rem(i, 8)
            for r0 in (0, 4):
                acc = first(pair, kb, r0)
                for j in range(2):
                    acc = madd(
                        acc,
                        lambda ms: e_ref[:, ms, pl.ds(j * LANES, LANES)],
                        lambda rs, ms: gath[pair * 2 + j, rs, ms, :],
                        KB, r0, 4)
                last(pair, kb, r0, acc)

        spread(0, e0)

        def two(h, _):
            spread(2 * h + 1, e1)
            step(2 * h, e0)
            spread(2 * h + 2, e0)
            step(2 * h + 1, e1)
            return 0

        lax.fori_loop(0, 16, two, 0)

    for c in shifts:
        c.wait_recv()
    for o in range(1, NDEV):
        leaf_copy(o).wait_recv()
    turned(recv)
    gather(lambda b: idx_ref[16 + lax.rem(b, 2) * 4 + b // 2])
    for t in range(TILES):
        for j in range(2):
            hots[t, :, pl.ds(j * LANES, LANES)] = hot(NOPS, idx_ref[24 + 4 * j + t])
    l_load.wait()

    def leaf_last(t, kb, r0, acc):
        lacc[t, pl.ds(r0, 4), pl.ds(pl.multiple_of(kb * 64, 64), 64), :] = acc.reshape(4, 64, LANES)

    coupling(lops, lambda t, kb, r0: None, leaf_last)

    for o in range(1, NDEV):
        parent_copy(o).wait_recv()
    turned(pbuf)
    gather(lambda b: idx_ref[32 + b])
    for b in range(8):
        hots[b // 2, :, pl.ds((b % 2) * LANES, LANES)] = hot(NOPS, idx_ref[40 + b])
    p_load.wait()
    pacc[...] = jnp.zeros_like(pacc)

    def pacc_at(kb, r0):
        return pl.ds(r0, 4), pl.ds(pl.multiple_of(kb * 64, 64), 64)

    def parent_first(pair, kb, r0):
        rs, ks = pacc_at(kb, r0)
        return pacc[rs, ks, :].reshape(4, KB, 8, LANES)

    def parent_last(pair, kb, r0, acc):
        rs, ks = pacc_at(kb, r0)
        pacc[rs, ks, :] = acc.reshape(4, 64, LANES)

    coupling(pops, parent_first, parent_last)

    for r in range(NRHS):
        for kb in range(8):
            total = None
            for s in range(8):
                v = pacc[r, pl.ds(kb * 64 + s, 8, stride=8), :]
                total = v if total is None else total + v
            total = total + pltpu.roll(total, 64, 1)
            child[0, r, pl.ds(kb * 8, 8), :] = total
    field = child[0].reshape(ROW, LANES).astype(bf16)
    for t in range(TILES):
        q = lax.broadcasted_iota(i32, (LANES, LANES), 0)
        at = lax.broadcasted_iota(i32, (LANES, LANES), 1) // 8 + t * 16
        wide = jnp.where(at == q, 1.0, 0.0).astype(bf16)
        gath[t] = dot(field, wide).reshape(NRHS, RANK, LANES)

    def down(mats, vecs, start, put):
        def step(i, _):
            t, kb = i // 8, lax.rem(i, 8)
            for r0 in (0, 4):
                rs, ks = pl.ds(r0, 4), pl.ds(pl.multiple_of(kb * 64, 64), 64)
                acc = madd(
                    start[t, rs, ks, :].reshape(4, KB, 8, LANES),
                    lambda ms: mats[pl.ds(pl.multiple_of(kb * KB, KB), KB), ms, lanes(t)],
                    lambda rs, ms: vecs[t, rs, ms, :],
                    KB, r0, 4)
                part[rs, :, :] = acc.reshape(4, 64, LANES)
            settle(part, put, (t, kb))
            return 0

        lax.fori_loop(0, 32, step, 0)

    def put_child(pos, r, v):
        t, kb = pos
        child[t, r, pl.ds(pl.multiple_of(kb * 8, 8), 8), :] = v.astype(bf16).astype(f32)

    down(trans, gath, lacc, put_child)

    def put_far(pos, r, v):
        t, kb = pos
        xf[t, r, pl.ds(pl.multiple_of(kb * 8, 8), 8), :] = v

    down(basis, child, nacc, put_far)
    for t in range(TILES):
        out_ref[pl.ds(t * LANES, LANES), :] = jnp.transpose(xf[t].reshape(ROW, LANES)).astype(bf16)

    for c in (*rims, *shifts):
        c.wait_send()
    for o in range(1, NDEV):
        leaf_copy(o).wait_send()
        parent_copy(o).wait_send()


def shards(rhs, basis, transfer, near_blocks, near_off, xch_idx, shift_idx, leaf_slot, leaf_op, parent_slot, parent_op, leaf_ops, parent_ops):
    row = lambda a: a.reshape(-1, LEAVES)
    idx = jnp.concatenate(
        [near_off.T, row(xch_idx), row(shift_idx), leaf_slot.T, leaf_op.T, row(parent_slot.T), row(parent_op.T)],
        axis=0).reshape(48, 1, LANES)
    anywhere = pl.BlockSpec(memory_space=pl.ANY)
    vmem = pl.BlockSpec(memory_space=pltpu.VMEM)
    tile = (TILES, NRHS, RANK, LANES)
    return pl.pallas_call(
        body,
        out_shape=jax.ShapeDtypeStruct((LEAVES, ROW), bf16),
        in_specs=[anywhere] * 6 + [vmem] * 2,
        out_specs=vmem,
        scratch_shapes=[
            pltpu.VMEM((64, 64, LEAVES), bf16),
            pltpu.VMEM((64, 64, LEAVES), bf16),
            pltpu.VMEM((2, 64, 64, LEAVES), bf16),
            pltpu.VMEM((64, 64, NOPS), bf16),
            pltpu.VMEM((64, 64, NOPS), bf16),
            pltpu.VMEM(tile, f32),
            pltpu.VMEM(tile, f32),
            pltpu.VMEM((NRHS, RANK, LEAVES), bf16),
            pltpu.VMEM((1024, ROW), bf16),
            pltpu.VMEM((1024, ROW), bf16),
            pltpu.VMEM((ROW, 1024), bf16),
            pltpu.VMEM((1024, ROW), bf16),
            pltpu.VMEM((2, 16, ROW), bf16),
            pltpu.VMEM((4, NOPS, 2 * LANES), bf16),
            pltpu.VMEM((8, NRHS, RANK, LANES), f32),
            pltpu.VMEM((TILES, NRHS, 512, LANES), f32),
            pltpu.VMEM((TILES, NRHS, 512, LANES), f32),
            pltpu.VMEM((NRHS, 512, LANES), f32),
            pltpu.VMEM((KB, RANK, 2 * LANES), f32),
            pltpu.VMEM((KB, RANK, 2 * LANES), f32),
            pltpu.VMEM((NRHS, 64, LANES), f32),
            pltpu.VMEM(tile, f32),
            pltpu.SemaphoreType.DMA((9,)),
            pltpu.SemaphoreType.DMA((34,)),
            pltpu.SemaphoreType.DMA((34,)),
        ],
        compiler_params=pltpu.CompilerParams(
            collective_id=0, has_side_effects=True, vmem_limit_bytes=62 << 20
        ),
        name="product",
    )(
        basis.transpose(1, 2, 0),
        transfer.transpose(1, 2, 0),
        near_blocks.transpose(1, 2, 3, 0),
        leaf_ops.transpose(1, 2, 0),
        parent_ops.transpose(1, 2, 0),
        rhs,
        rhs.T,
        idx,
    )


def solution(mesh):
    spec = P(("group", "dev"))
    return jax.shard_map(
        shards,
        mesh=mesh,
        in_specs=(spec,) * 11 + (P(), P()),
        out_specs=spec,
        check_vma=False,
    )
```

profile of v0, /device:TPU:0, one launch (start us, length us, event | category | flops | bytes accessed | tf_op | source)
XLA Modules:
  0.0 107.0 jit_solution(5493048458983318953)
XLA Ops:
  0.0 0.8 reshape.17
  0.8 0.8 reshape.18
  1.5 0.8 concatenate.3
  2.3 0.6 reshape.19.idx_ref
  3.0 2.0 %copy.14 = bf16[512,512]{0,1:T(8,128)(2,1)} copy(bf16[512,512]{1,0:T(8,128)(2,1)} %rhs_h.1) | data formatting | bytes 1048576 | tf_op args[0]
  5.0 100.2 %product.1 = bf16[512,512]{1,0:T(8,128)(2,1)} custom-call(bf16[64,64,512]{2,1,0:T(8,128)(2,1)} %bitcast.14, bf16[64,64,512]{2,1,0:T(8,128)(2,1)} %bitcast.15, bf16[2,64,64,512]{3,2,1,0:T(8,128)(2,1)} %bitcast.13, bf16[64,64,316]{2,1,0:T(8,128)(2,1)} %bitcast.16, bf16[64,64,316]{2,1,0:T(8,128)(2,1)} %bitcast.17, bf16[512,512]{1,0:T(8,128)(2,1)} %rhs_h.1, ...), custom_call_target="tpu_custom_call" | custom-call | tf_op jit(solution)/shard_map/product/pallas_call | solution.py:377
  105.2 1.9 %copy.16 = bf16[512,512]{1,0:T(8,128)(2,1)} copy(bf16[512,512]{1,0:T(8,128)(2,1)} %product.1) | data formatting | bytes 1048576
where the time goes:
time: 107 us
  Pallas kernels  100 us (93%)
  local copies, waits for them, and re-layouts  6.88 us (6%)
    pallas_call x1, Pallas kernels, shards(): pl.pallas_call(body, out_shape=jax.ShapeDtypeStruct((LEAVES, ROW), bf16),...  100 us
    unnamed x2, local copies, waits for them, and re-layouts  3.91 us

commit v1 on v0

--- a/solution.py
+++ b/solution.py
@@ -65,7 +65,7 @@
     lax.fori_loop(0, 2 * TILES, tile, 0)
 
 
-def madd(acc, mats, vecs, width, r0, rb):
+def madd(acc, mats, vecs, r0, rb):
     for mp in range(4):
         a = mats(pl.ds(mp * 16, 16)).astype(f32)
         for h in range(2):
@@ -75,19 +75,22 @@
     return acc
 
 
-def settle(part, out, pos):
-    for r in range(NRHS):
-        total = None
-        for s in range(8):
-            v = part[r, pl.ds(s, KB, stride=8), :]
-            total = v if total is None else total + v
-        out(pos, r, total)
+def settle(acc):
+    row = lax.broadcasted_iota(i32, (1, 1, 8, LANES), 2)
+    for bit in (1, 2, 4):
+        n = acc.shape[1] // 2
+        pairs = acc.reshape(acc.shape[0], n, 2, 8, LANES)
+        a, b = pairs[:, :, 0], pairs[:, :, 1]
+        own = (row & bit) == 0
+        x, y = jnp.where(own, a, b), jnp.where(own, b, a)
+        acc = x + pltpu.roll(y, 8 - bit, 2)
+    return acc[:, 0]
 
 
 def body(
-    basis_h, trans_h, near_h, lops_h, pops_h, rhs_h, xt_ref, idx_ref, out_ref,
-    basis, trans, near, lops, pops, xf, lcf, lcb, send, recv, recvt, pbuf, rim, hots,
-    gath, nacc, lacc, pacc, e0, e1, part, child, load, tx, rx,
+    basis_h, trans_h, near_h, lops_h, pops_h, rhs_ref, off_ref, xch_ref, shift_ref, lslot_ref, lop_ref, pslot_ref, pop_ref, out_ref,
+    idx_ref, xt_ref, basis, trans, near, lops, pops, xf, lcf, lcb, send, recv, recvt, pbuf, rim, hots,
+    gath, nacc, lacc, pacc, mats, child, load, tx, rx,
 ):
     g, me = lax.axis_index("group"), lax.axis_index("dev")
     n_group = lax.axis_size("group")
@@ -112,7 +115,24 @@
         pl.semaphore_signal(barrier, inc=1, device_id={"group": other}, device_id_type=MESH)
 
     for t in range(TILES):
-        xf[t] = xt_ref[:, pl.ds(t * LANES, LANES)].astype(f32).reshape(NRHS, RANK, LANES)
+        cut = pl.ds(t * LANES, LANES)
+        for j in range(2):
+            idx_ref[4 * j + t] = off_ref[pl.ds(j, 1), cut]
+            idx_ref[16 + 4 * j + t] = lslot_ref[pl.ds(j, 1), cut]
+            idx_ref[24 + 4 * j + t] = lop_ref[pl.ds(j, 1), cut]
+        idx_ref[8 + t] = xch_ref[:, cut]
+        idx_ref[12 + t] = shift_ref[:, cut]
+    for b in range(8):
+        for first, ref in ((32, pslot_ref), (40, pop_ref)):
+            idx_ref[first + b] = jnp.concatenate([ref[pl.ds(2 * b, 1), :], ref[pl.ds(2 * b + 1, 1), :]], axis=1)
+
+    def turn_x(t, _):
+        v = jnp.transpose(rhs_ref[lanes(t), :].astype(f32))
+        xt_ref[:, lanes(t)] = v.astype(bf16)
+        xf[t] = v.reshape(NRHS, RANK, LANES)
+        return 0
+
+    lax.fori_loop(0, TILES, turn_x, 0)
 
     def put_leaf(t, r, ks, v):
         b = v.astype(bf16)
@@ -128,21 +148,24 @@
 
     upward(basis, xf, put_leaf, wait_basis)
 
-    def pick(b, _):
-        row = idx_ref[8 + b].astype(f32)
-        col = jnp.transpose(jnp.broadcast_to(row, (LANES, LANES)))
+    def pick(h, _):
         at = lax.broadcasted_iota(i32, (LANES, LANES), 1).astype(f32)
-        pieces = [jnp.where(at + float(t * LANES) == col, 1.0, 0.0).astype(bf16) for t in range(TILES)]
-        chosen = dot(jnp.concatenate(pieces, axis=1), lcb[...].reshape(ROW, LEAVES), ((1,), (1,)))
-        send[pl.ds(pl.multiple_of(b * LANES, LANES), LANES), :] = chosen.astype(bf16)
+        rows = []
+        for b in range(4):
+            row = idx_ref[8 + h * 4 + b].astype(f32)
+            col = jnp.transpose(jnp.broadcast_to(row, (LANES, LANES)))
+            pieces = [jnp.where(at + float(t * LANES) == col, 1.0, 0.0).astype(bf16) for t in range(TILES)]
+            rows.append(jnp.concatenate(pieces, axis=1))
+        chosen = dot(jnp.concatenate(rows, axis=0), lcb[...].reshape(ROW, LEAVES), ((1,), (1,)))
+        send[pl.ds(pl.multiple_of(h * 512, 512), 512), :] = chosen.astype(bf16)
         return 0
 
-    lax.fori_loop(0, 8, pick, 0)
+    lax.fori_loop(0, 2, pick, 0)
 
     pl.semaphore_wait(barrier, NDEV + 1)
     rims = [
         pltpu.make_async_remote_copy(
-            src_ref=rhs_h.at[pl.ds(first, 16)], dst_ref=rim.at[s], send_sem=tx.at[32 + s], recv_sem=rx.at[32 + s],
+            src_ref=rhs_ref.at[pl.ds(first, 16)], dst_ref=rim.at[s], send_sem=tx.at[32 + s], recv_sem=rx.at[32 + s],
             device_id={"dev": to}, device_id_type=MESH)
         for s, first, to in ((0, LEAVES - 16, right), (1, 0, left))
     ]
@@ -199,20 +222,22 @@
     rim_rows = jnp.concatenate([rim[0], rim[1]], axis=0)
     rim_t = jnp.transpose(rim_rows.astype(f32)).astype(bf16)
 
-    def partners(b, _):
-        j, t = b // TILES, lax.rem(b, TILES)
-        off = idx_ref[b]
-        leaf = lax.broadcasted_iota(i32, (1, LANES), 1) + t * LANES + off - REACH
+    def partners(h, _):
+        j = h // 2
+        first = lax.rem(h, 2) * 2
+        off = jnp.concatenate([idx_ref[2 * h], idx_ref[2 * h + 1]], axis=1)
+        leaf = lax.broadcasted_iota(i32, (1, 2 * LANES), 1) + first * LANES + off - REACH
         leaf = jnp.where((me == 0) & (leaf < 0), -100, leaf)
         leaf = jnp.where((me == NDEV - 1) & (leaf >= LEAVES), -100, leaf)
-        at = lax.broadcasted_iota(i32, (32, LANES), 0)
+        at = lax.broadcasted_iota(i32, (32, 2 * LANES), 0)
         at = jnp.where(at < 16, at - 16, at + (LEAVES - 16))
         edge = jnp.where(at == leaf, 1.0, 0.0).astype(bf16)
         v = dot(xt_ref[...], hot(LEAVES, leaf)) + dot(rim_t, edge)
-        gath[b] = v.reshape(NRHS, RANK, LANES)
+        gath[2 * h] = v[:, :LANES].reshape(NRHS, RANK, LANES)
+        gath[2 * h + 1] = v[:, LANES:].reshape(NRHS, RANK, LANES)
         return 0
 
-    lax.fori_loop(0, 8, partners, 0)
+    lax.fori_loop(0, 4, partners, 0)
     for c in n_loads:
         c.wait()
 
@@ -225,7 +250,7 @@
                     acc,
                     lambda ms: near[j, pl.ds(pl.multiple_of(kb * KB, KB), KB), ms, lanes(t)],
                     lambda rs, ms: gath[j * TILES + t, rs, ms, :],
-                    KB, r0, 4)
+                    r0, 4)
             nacc[t, pl.ds(r0, 4), pl.ds(pl.multiple_of(kb * 64, 64), 64), :] = acc.reshape(4, 64, LANES)
         return 0
 
@@ -240,41 +265,36 @@
         lax.fori_loop(0, 8, block, 0)
 
     def gather(row_of):
-        def block(b, _):
-            gath[b] = dot(recvt[...], hot(1024, row_of(b))).reshape(NRHS, RANK, LANES)
+        def block(h, _):
+            rows = jnp.concatenate([row_of(2 * h), row_of(2 * h + 1)], axis=1)
+            v = dot(recvt[...], hot(1024, rows))
+            gath[2 * h] = v[:, :LANES].reshape(NRHS, RANK, LANES)
+            gath[2 * h + 1] = v[:, LANES:].reshape(NRHS, RANK, LANES)
             return 0
 
-        lax.fori_loop(0, 8, block, 0)
-
-    def coupling(ops, first, last):
-        def spread(i, e_ref):
-            i = jnp.minimum(i, 31)
-            pair, kb = i // 8, lax.rem(i, 8)
-            rows = ops[pl.ds(pl.multiple_of(kb * KB, KB), KB)].reshape(KB * RANK, NOPS)
-            e_ref[...] = dot(rows, hots[pair]).reshape(KB, RANK, 2 * LANES)
-
-        def step(i, e_ref):
-            pair, kb = i // 8, lax.rem(i, 8)
-            for r0 in (0, 4):
-                acc = first(pair, kb, r0)
-                for j in range(2):
-                    acc = madd(
-                        acc,
-                        lambda ms: e_ref[:, ms, pl.ds(j * LANES, LANES)],
-                        lambda rs, ms: gath[pair * 2 + j, rs, ms, :],
-                        KB, r0, 4)
-                last(pair, kb, r0, acc)
-
-        spread(0, e0)
-
-        def two(h, _):
-            spread(2 * h + 1, e1)
-            step(2 * h, e0)
-            spread(2 * h + 2, e0)
-            step(2 * h + 1, e1)
+        lax.fori_loop(0, 4, block, 0)
+
+    def coupling(ops, last):
+        def pair_of(pair, _):
+            v = dot(ops[...].reshape(RANK * RANK, NOPS), hots[pair])
+            mats[...] = v.astype(bf16).reshape(RANK, RANK, 2 * LANES)
+
+            def step(kb, _):
+                for r0 in (0, 4):
+                    acc = None
+                    for j in range(2):
+                        acc = madd(
+                            acc,
+                            lambda ms: mats[pl.ds(pl.multiple_of(kb * KB, KB), KB), ms, pl.ds(j * LANES, LANES)],
+                            lambda rs, ms: gath[pair * 2 + j, rs, ms, :],
+                            r0, 4)
+                    last(pair, kb, r0, acc)
+                return 0
+
+            lax.fori_loop(0, 8, step, 0)
             return 0
 
-        lax.fori_loop(0, 16, two, 0)
+        lax.fori_loop(0, 4, pair_of, 0)
 
     for c in shifts:
         c.wait_recv()
@@ -290,7 +310,7 @@
     def leaf_last(t, kb, r0, acc):
         lacc[t, pl.ds(r0, 4), pl.ds(pl.multiple_of(kb * 64, 64), 64), :] = acc.reshape(4, 64, LANES)
 
-    coupling(lops, lambda t, kb, r0: None, leaf_last)
+    coupling(lops, leaf_last)
 
     for o in range(1, NDEV):
         parent_copy(o).wait_recv()
@@ -304,24 +324,15 @@
     def pacc_at(kb, r0):
         return pl.ds(r0, 4), pl.ds(pl.multiple_of(kb * 64, 64), 64)
 
-    def parent_first(pair, kb, r0):
-        rs, ks = pacc_at(kb, r0)
-        return pacc[rs, ks, :].reshape(4, KB, 8, LANES)
-
     def parent_last(pair, kb, r0, acc):
         rs, ks = pacc_at(kb, r0)
-        pacc[rs, ks, :] = acc.reshape(4, 64, LANES)
-
-    coupling(pops, parent_first, parent_last)
-
-    for r in range(NRHS):
-        for kb in range(8):
-            total = None
-            for s in range(8):
-                v = pacc[r, pl.ds(kb * 64 + s, 8, stride=8), :]
-                total = v if total is None else total + v
-            total = total + pltpu.roll(total, 64, 1)
-            child[0, r, pl.ds(kb * 8, 8), :] = total
+        pacc[rs, ks, :] += acc.reshape(4, 64, LANES)
+
+    coupling(pops, parent_last)
+
+    for kb in range(8):
+        total = settle(pacc[:, pl.ds(kb * 64, 64), :].reshape(NRHS, KB, 8, LANES))
+        child[0, :, pl.ds(kb * 8, 8), :] = total + pltpu.roll(total, 64, 2)
     field = child[0].reshape(ROW, LANES).astype(bf16)
     for t in range(TILES):
         q = lax.broadcasted_iota(i32, (LANES, LANES), 0)
@@ -338,22 +349,21 @@
                     start[t, rs, ks, :].reshape(4, KB, 8, LANES),
                     lambda ms: mats[pl.ds(pl.multiple_of(kb * KB, KB), KB), ms, lanes(t)],
                     lambda rs, ms: vecs[t, rs, ms, :],
-                    KB, r0, 4)
-                part[rs, :, :] = acc.reshape(4, 64, LANES)
-            settle(part, put, (t, kb))
+                    r0, 4)
+                put((t, kb), rs, settle(acc))
             return 0
 
         lax.fori_loop(0, 32, step, 0)
 
-    def put_child(pos, r, v):
+    def put_child(pos, rs, v):
         t, kb = pos
-        child[t, r, pl.ds(pl.multiple_of(kb * 8, 8), 8), :] = v.astype(bf16).astype(f32)
+        child[t, rs, pl.ds(pl.multiple_of(kb * 8, 8), 8), :] = v.astype(bf16).astype(f32)
 
     down(trans, gath, lacc, put_child)
 
-    def put_far(pos, r, v):
+    def put_far(pos, rs, v):
         t, kb = pos
-        xf[t, r, pl.ds(pl.multiple_of(kb * 8, 8), 8), :] = v
+        xf[t, rs, pl.ds(pl.multiple_of(kb * 8, 8), 8), :] = v
 
     down(basis, child, nacc, put_far)
     for t in range(TILES):
@@ -367,19 +377,17 @@
 
 
 def shards(rhs, basis, transfer, near_blocks, near_off, xch_idx, shift_idx, leaf_slot, leaf_op, parent_slot, parent_op, leaf_ops, parent_ops):
-    row = lambda a: a.reshape(-1, LEAVES)
-    idx = jnp.concatenate(
-        [near_off.T, row(xch_idx), row(shift_idx), leaf_slot.T, leaf_op.T, row(parent_slot.T), row(parent_op.T)],
-        axis=0).reshape(48, 1, LANES)
     anywhere = pl.BlockSpec(memory_space=pl.ANY)
     vmem = pl.BlockSpec(memory_space=pltpu.VMEM)
     tile = (TILES, NRHS, RANK, LANES)
     return pl.pallas_call(
         body,
         out_shape=jax.ShapeDtypeStruct((LEAVES, ROW), bf16),
-        in_specs=[anywhere] * 6 + [vmem] * 2,
+        in_specs=[anywhere] * 5 + [vmem] * 8,
         out_specs=vmem,
         scratch_shapes=[
+            pltpu.VMEM((48, 1, LANES), i32),
+            pltpu.VMEM((ROW, LEAVES), bf16),
             pltpu.VMEM((64, 64, LEAVES), bf16),
             pltpu.VMEM((64, 64, LEAVES), bf16),
             pltpu.VMEM((2, 64, 64, LEAVES), bf16),
@@ -398,9 +406,7 @@
             pltpu.VMEM((TILES, NRHS, 512, LANES), f32),
             pltpu.VMEM((TILES, NRHS, 512, LANES), f32),
             pltpu.VMEM((NRHS, 512, LANES), f32),
-            pltpu.VMEM((KB, RANK, 2 * LANES), f32),
-            pltpu.VMEM((KB, RANK, 2 * LANES), f32),
-            pltpu.VMEM((NRHS, 64, LANES), f32),
+            pltpu.VMEM((RANK, RANK, 2 * LANES), bf16),
             pltpu.VMEM(tile, f32),
             pltpu.SemaphoreType.DMA((9,)),
             pltpu.SemaphoreType.DMA((34,)),
@@ -417,8 +423,13 @@
         leaf_ops.transpose(1, 2, 0),
         parent_ops.transpose(1, 2, 0),
         rhs,
-        rhs.T,
-        idx,
+        near_off.T,
+        xch_idx.reshape(1, LEAVES),
+        shift_idx.reshape(1, LEAVES),
+        leaf_slot.T,
+        leaf_op.T,
+        parent_slot.T,
+        parent_op.T,
     )
 
 

time: 107 us -> 84.4 us (0.79)
  Pallas kernels: 100 us -> 82.4 us
  local copies, waits for them, and re-layouts: 6.88 us -> 1.87 us
    pallas_call x1, Pallas kernels: 100 us -> 82.4 us  [shards(): pl.pallas_call(body, out_shape=jax.ShapeDtypeStruct((LEAVES, ROW), bf16),...]
    reshape x3 -> x0, local copies, waits for them, and re-layouts: 2.17 us -> none  [the longest x2 1.54 us: shards(): row = lambda a: a.reshape(-1, LEAVES)]
    unnamed x2 -> x1, local copies, waits for them, and re-layouts: 3.91 us -> 1.87 us
where the time goes in v1:
time: 84.4 us; the launch traced here: 84.3 us
  Pallas kernels  82.4 us (98%)
  local copies, waits for them, and re-layouts  1.87 us (2%)
    pallas_call x1, Pallas kernels, shards(): pl.pallas_call(body, out_shape=jax.ShapeDtypeStruct((LEAVES, ROW), bf16),...  82.4 us
    unnamed x1, local copies, waits for them, and re-layouts  1.87 us

profile of v1, /device:TPU:0, one launch (start us, length us, event | category | flops | bytes accessed | tf_op | source)
XLA Modules:
  0.0 84.3 jit_solution(14584375289858112459)
XLA Ops:
  0.0 82.4 %product.1 = bf16[512,512]{1,0:T(8,128)(2,1)} custom-call(bf16[64,64,512]{2,1,0:T(8,128)(2,1)} %bitcast.13, bf16[64,64,512]{2,1,0:T(8,128)(2,1)} %bitcast.14, bf16[2,64,64,512]{3,2,1,0:T(8,128)(2,1)} %bitcast.12, bf16[64,64,316]{2,1,0:T(8,128)(2,1)} %bitcast.15, bf16[64,64,316]{2,1,0:T(8,128)(2,1)} %bitcast.16, bf16[512,512]{1,0:T(8,128)(2,1)} %rhs_ref.1, ...), custom_call_target="tpu_custom_call" | custom-call | tf_op jit(solution)/shard_map/product/pallas_call | solution.py:383
  82.4 1.9 %copy.15 = bf16[512,512]{1,0:T(8,128)(2,1)} copy(bf16[512,512]{1,0:T(8,128)(2,1)} %product.1) | data formatting | bytes 1048576

commit v2 on v1

--- a/solution.py
+++ b/solution.py
@@ -75,6 +75,14 @@
     return acc
 
 
+def madd8(acc, mats, vecs, r0, rb):
+    for m in range(8):
+        rows = pl.ds(m * 8, 8)
+        v = mats(rows)[None] * vecs(pl.ds(r0, rb), rows)[:, None]
+        acc = v if acc is None else acc + v
+    return acc
+
+
 def settle(acc):
     row = lax.broadcasted_iota(i32, (1, 1, 8, LANES), 2)
     for bit in (1, 2, 4):
@@ -90,7 +98,7 @@
 def body(
     basis_h, trans_h, near_h, lops_h, pops_h, rhs_ref, off_ref, xch_ref, shift_ref, lslot_ref, lop_ref, pslot_ref, pop_ref, out_ref,
     idx_ref, xt_ref, basis, trans, near, lops, pops, xf, lcf, lcb, send, recv, recvt, pbuf, rim, hots,
-    gath, nacc, lacc, pacc, mats, child, load, tx, rx,
+    gath, nacc, lacc, pacc, mats, wide, load, tx, rx,
 ):
     g, me = lax.axis_index("group"), lax.axis_index("dev")
     n_group = lax.axis_size("group")
@@ -129,7 +137,7 @@
     def turn_x(t, _):
         v = jnp.transpose(rhs_ref[lanes(t), :].astype(f32))
         xt_ref[:, lanes(t)] = v.astype(bf16)
-        xf[t] = v.reshape(NRHS, RANK, LANES)
+        xf[t, :, pl.ds(0, RANK), :] = v.reshape(NRHS, RANK, LANES)
         return 0
 
     lax.fori_loop(0, TILES, turn_x, 0)
@@ -200,7 +208,7 @@
     t_load.wait()
 
     def put_parent(t, r, ks, v):
-        child[t, r, ks, :] = v
+        xf[t, r, ks, :] = v
 
     upward(trans, lcf, put_parent, lambda i: None)
     at = lax.broadcasted_iota(i32, (PAR, LANES), 1) // 8
@@ -208,7 +216,7 @@
     total = None
     for t in range(TILES):
         pool = jnp.where(at + t * 16 == q, 1.0, 0.0).astype(bf16)
-        v = child[t].reshape(ROW, LANES)
+        v = xf[t, :, pl.ds(0, RANK), :].reshape(ROW, LANES)
         high = v.astype(bf16)
         low = (v - high.astype(f32)).astype(bf16)
         s = dot(pool, high, ((1,), (1,))) + dot(pool, low, ((1,), (1,)))
@@ -222,35 +230,31 @@
     rim_rows = jnp.concatenate([rim[0], rim[1]], axis=0)
     rim_t = jnp.transpose(rim_rows.astype(f32)).astype(bf16)
 
-    def partners(h, _):
-        j = h // 2
-        first = lax.rem(h, 2) * 2
-        off = jnp.concatenate([idx_ref[2 * h], idx_ref[2 * h + 1]], axis=1)
-        leaf = lax.broadcasted_iota(i32, (1, 2 * LANES), 1) + first * LANES + off - REACH
+    def partners(j, _):
+        off = jnp.concatenate([idx_ref[4 * j + t] for t in range(TILES)], axis=1)
+        leaf = lax.broadcasted_iota(i32, (1, LEAVES), 1) + off - REACH
         leaf = jnp.where((me == 0) & (leaf < 0), -100, leaf)
         leaf = jnp.where((me == NDEV - 1) & (leaf >= LEAVES), -100, leaf)
-        at = lax.broadcasted_iota(i32, (32, 2 * LANES), 0)
+        at = lax.broadcasted_iota(i32, (32, LEAVES), 0)
         at = jnp.where(at < 16, at - 16, at + (LEAVES - 16))
         edge = jnp.where(at == leaf, 1.0, 0.0).astype(bf16)
         v = dot(xt_ref[...], hot(LEAVES, leaf)) + dot(rim_t, edge)
-        gath[2 * h] = v[:, :LANES].reshape(NRHS, RANK, LANES)
-        gath[2 * h + 1] = v[:, LANES:].reshape(NRHS, RANK, LANES)
+        for t in range(TILES):
+            gath[j * TILES + t] = v[:, t * LANES : (t + 1) * LANES].reshape(NRHS, RANK, LANES)
         return 0
 
-    lax.fori_loop(0, 4, partners, 0)
+    lax.fori_loop(0, 2, partners, 0)
     for c in n_loads:
         c.wait()
 
     def near_step(i, _):
         t, kb = i // 8, lax.rem(i, 8)
+        for j in range(2):
+            wide[j] = near[j, pl.ds(pl.multiple_of(kb * KB, KB), KB), :, lanes(t)].astype(f32)
         for r0 in (0, 4):
             acc = None
             for j in range(2):
-                acc = madd(
-                    acc,
-                    lambda ms: near[j, pl.ds(pl.multiple_of(kb * KB, KB), KB), ms, lanes(t)],
-                    lambda rs, ms: gath[j * TILES + t, rs, ms, :],
-                    r0, 4)
+                acc = madd8(acc, lambda ms: wide[j, :, ms, :], lambda rs, ms: gath[j * TILES + t, rs, ms, :], r0, 4)
             nacc[t, pl.ds(r0, 4), pl.ds(pl.multiple_of(kb * 64, 64), 64), :] = acc.reshape(4, 64, LANES)
         return 0
 
@@ -266,18 +270,18 @@
 
     def gather(row_of):
         def block(h, _):
-            rows = jnp.concatenate([row_of(2 * h), row_of(2 * h + 1)], axis=1)
+            rows = jnp.concatenate([row_of(4 * h + b) for b in range(4)], axis=1)
             v = dot(recvt[...], hot(1024, rows))
-            gath[2 * h] = v[:, :LANES].reshape(NRHS, RANK, LANES)
-            gath[2 * h + 1] = v[:, LANES:].reshape(NRHS, RANK, LANES)
+            for b in range(4):
+                gath[4 * h + b] = v[:, b * LANES : (b + 1) * LANES].reshape(NRHS, RANK, LANES)
             return 0
 
-        lax.fori_loop(0, 4, block, 0)
+        lax.fori_loop(0, 2, block, 0)
 
     def coupling(ops, last):
         def pair_of(pair, _):
             v = dot(ops[...].reshape(RANK * RANK, NOPS), hots[pair])
-            mats[...] = v.astype(bf16).reshape(RANK, RANK, 2 * LANES)
+            mats[...] = v.reshape(RANK, RANK, 2 * LANES)
 
             def step(kb, _):
                 for r0 in (0, 4):
@@ -332,13 +336,13 @@
 
     for kb in range(8):
         total = settle(pacc[:, pl.ds(kb * 64, 64), :].reshape(NRHS, KB, 8, LANES))
-        child[0, :, pl.ds(kb * 8, 8), :] = total + pltpu.roll(total, 64, 2)
-    field = child[0].reshape(ROW, LANES).astype(bf16)
+        lcf[0, :, pl.ds(kb * 8, 8), :] = total + pltpu.roll(total, 64, 2)
+    field = lcf[0, :, pl.ds(0, RANK), :].reshape(ROW, LANES).astype(bf16)
     for t in range(TILES):
         q = lax.broadcasted_iota(i32, (LANES, LANES), 0)
         at = lax.broadcasted_iota(i32, (LANES, LANES), 1) // 8 + t * 16
-        wide = jnp.where(at == q, 1.0, 0.0).astype(bf16)
-        gath[t] = dot(field, wide).reshape(NRHS, RANK, LANES)
+        ones = jnp.where(at == q, 1.0, 0.0).astype(bf16)
+        gath[t] = dot(field, ones).reshape(NRHS, RANK, LANES)
 
     def down(mats, vecs, start, put):
         def step(i, _):
@@ -357,7 +361,7 @@
 
     def put_child(pos, rs, v):
         t, kb = pos
-        child[t, rs, pl.ds(pl.multiple_of(kb * 8, 8), 8), :] = v.astype(bf16).astype(f32)
+        lcf[t, rs, pl.ds(pl.multiple_of(kb * 8, 8), 8), :] = v.astype(bf16).astype(f32)
 
     down(trans, gath, lacc, put_child)
 
@@ -365,9 +369,9 @@
         t, kb = pos
         xf[t, rs, pl.ds(pl.multiple_of(kb * 8, 8), 8), :] = v
 
-    down(basis, child, nacc, put_far)
+    down(basis, lcf, nacc, put_far)
     for t in range(TILES):
-        out_ref[pl.ds(t * LANES, LANES), :] = jnp.transpose(xf[t].reshape(ROW, LANES)).astype(bf16)
+        out_ref[pl.ds(t * LANES, LANES), :] = jnp.transpose(xf[t, :, pl.ds(0, RANK), :].reshape(ROW, LANES)).astype(bf16)
 
     for c in (*rims, *shifts):
         c.wait_send()
@@ -379,7 +383,7 @@
 def shards(rhs, basis, transfer, near_blocks, near_off, xch_idx, shift_idx, leaf_slot, leaf_op, parent_slot, parent_op, leaf_ops, parent_ops):
     anywhere = pl.BlockSpec(memory_space=pl.ANY)
     vmem = pl.BlockSpec(memory_space=pltpu.VMEM)
-    tile = (TILES, NRHS, RANK, LANES)
+    padded = (TILES, NRHS, RANK + 8, LANES)
     return pl.pallas_call(
         body,
         out_shape=jax.ShapeDtypeStruct((LEAVES, ROW), bf16),
@@ -393,8 +397,8 @@
             pltpu.VMEM((2, 64, 64, LEAVES), bf16),
             pltpu.VMEM((64, 64, NOPS), bf16),
             pltpu.VMEM((64, 64, NOPS), bf16),
-            pltpu.VMEM(tile, f32),
-            pltpu.VMEM(tile, f32),
+            pltpu.VMEM(padded, f32),
+            pltpu.VMEM(padded, f32),
             pltpu.VMEM((NRHS, RANK, LEAVES), bf16),
             pltpu.VMEM((1024, ROW), bf16),
             pltpu.VMEM((1024, ROW), bf16),
@@ -406,14 +410,14 @@
             pltpu.VMEM((TILES, NRHS, 512, LANES), f32),
             pltpu.VMEM((TILES, NRHS, 512, LANES), f32),
             pltpu.VMEM((NRHS, 512, LANES), f32),
-            pltpu.VMEM((RANK, RANK, 2 * LANES), bf16),
-            pltpu.VMEM(tile, f32),
+            pltpu.VMEM((RANK, RANK, 2 * LANES), f32),
+            pltpu.VMEM((2, KB, RANK, LANES), f32),
             pltpu.SemaphoreType.DMA((9,)),
             pltpu.SemaphoreType.DMA((34,)),
             pltpu.SemaphoreType.DMA((34,)),
         ],
         compiler_params=pltpu.CompilerParams(
-            collective_id=0, has_side_effects=True, vmem_limit_bytes=62 << 20
+            collective_id=0, has_side_effects=True, vmem_limit_bytes=127 << 19
         ),
         name="product",
     )(

time: 84.4 us -> 79.5 us (0.942)
  Pallas kernels: 82.4 us -> 77.4 us
    pallas_call x1, Pallas kernels: 82.4 us -> 77.4 us  [shards(): pl.pallas_call(body, out_shape=jax.ShapeDtypeStruct((LEAVES, ROW), bf16),...]
where the time goes in v2:
time: 79.5 us; the launch traced here: 79.3 us
  Pallas kernels  77.4 us (97%)
  local copies, waits for them, and re-layouts  1.87 us (2%)
    pallas_call x1, Pallas kernels, shards(): pl.pallas_call(body, out_shape=jax.ShapeDtypeStruct((LEAVES, ROW), bf16),...  77.4 us
    unnamed x1, local copies, waits for them, and re-layouts  1.87 us

profile of v2, /device:TPU:0, one launch (start us, length us, event | category | flops | bytes accessed | tf_op | source)
XLA Modules:
  0.0 79.3 jit_solution(8410684281418860420)
XLA Ops:
  0.0 77.4 %product.1 = bf16[512,512]{1,0:T(8,128)(2,1)} custom-call(bf16[64,64,512]{2,1,0:T(8,128)(2,1)} %bitcast.13, bf16[64,64,512]{2,1,0:T(8,128)(2,1)} %bitcast.14, bf16[2,64,64,512]{3,2,1,0:T(8,128)(2,1)} %bitcast.12, bf16[64,64,316]{2,1,0:T(8,128)(2,1)} %bitcast.15, bf16[64,64,316]{2,1,0:T(8,128)(2,1)} %bitcast.16, bf16[512,512]{1,0:T(8,128)(2,1)} %rhs_ref.1, ...), custom_call_target="tpu_custom_call" | custom-call | tf_op jit(solution)/shard_map/product/pallas_call | solution.py:387
  77.4 1.9 %copy.15 = bf16[512,512]{1,0:T(8,128)(2,1)} copy(bf16[512,512]{1,0:T(8,128)(2,1)} %product.1) | data formatting | bytes 1048576

commit v3 on v2

--- a/solution.py
+++ b/solution.py
@@ -96,8 +96,8 @@
 
 
 def body(
-    basis_h, trans_h, near_h, lops_h, pops_h, rhs_ref, off_ref, xch_ref, shift_ref, lslot_ref, lop_ref, pslot_ref, pop_ref, out_ref,
-    idx_ref, xt_ref, basis, trans, near, lops, pops, xf, lcf, lcb, send, recv, recvt, pbuf, rim, hots,
+    basis_h, trans_h, near_h, lops_h, pops_h, rhs_h, off_ref, xch_ref, shift_ref, lslot_ref, lop_ref, pslot_ref, pop_ref, out_ref,
+    idx_ref, xt_ref, rhs_ref, basis, trans, near, lops, pops, xf, lcf, lcb, send, recv, recvt, pbuf, rim, hots,
     gath, nacc, lacc, pacc, mats, wide, load, tx, rx,
 ):
     g, me = lax.axis_index("group"), lax.axis_index("dev")
@@ -109,11 +109,12 @@
         pltpu.make_async_copy(basis_h.at[:, :, pl.ds(t * LANES, LANES)], basis.at[:, :, pl.ds(t * LANES, LANES)], load.at[t])
         for t in range(TILES)
     ]
+    x_load = pltpu.make_async_copy(rhs_h, rhs_ref, load.at[9])
     t_load = pltpu.make_async_copy(trans_h, trans, load.at[4])
     n_loads = [pltpu.make_async_copy(near_h.at[j], near.at[j], load.at[5 + j]) for j in range(2)]
     l_load = pltpu.make_async_copy(lops_h, lops, load.at[7])
     p_load = pltpu.make_async_copy(pops_h, pops, load.at[8])
-    for c in (*b_loads, t_load, *n_loads, l_load, p_load):
+    for c in (x_load, *b_loads, t_load, *n_loads, l_load, p_load):
         c.start()
 
     barrier = pltpu.get_barrier_semaphore()
@@ -140,6 +141,7 @@
         xf[t, :, pl.ds(0, RANK), :] = v.reshape(NRHS, RANK, LANES)
         return 0
 
+    x_load.wait()
     lax.fori_loop(0, TILES, turn_x, 0)
 
     def put_leaf(t, r, ks, v):
@@ -387,11 +389,12 @@
     return pl.pallas_call(
         body,
         out_shape=jax.ShapeDtypeStruct((LEAVES, ROW), bf16),
-        in_specs=[anywhere] * 5 + [vmem] * 8,
+        in_specs=[anywhere] * 6 + [vmem] * 7,
         out_specs=vmem,
         scratch_shapes=[
             pltpu.VMEM((48, 1, LANES), i32),
             pltpu.VMEM((ROW, LEAVES), bf16),
+            pltpu.VMEM((LEAVES, ROW), bf16),
             pltpu.VMEM((64, 64, LEAVES), bf16),
             pltpu.VMEM((64, 64, LEAVES), bf16),
             pltpu.VMEM((2, 64, 64, LEAVES), bf16),
@@ -412,7 +415,7 @@
             pltpu.VMEM((NRHS, 512, LANES), f32),
             pltpu.VMEM((RANK, RANK, 2 * LANES), f32),
             pltpu.VMEM((2, KB, RANK, LANES), f32),
-            pltpu.SemaphoreType.DMA((9,)),
+            pltpu.SemaphoreType.DMA((10,)),
             pltpu.SemaphoreType.DMA((34,)),
             pltpu.SemaphoreType.DMA((34,)),
         ],

time: 79.5 us -> 79.5 us (level)
  no operation moved by 1% of the time
where the time goes in v3:
time: 79.5 us; the launch traced here: 79.3 us
  Pallas kernels  77.4 us (97%)
  local copies, waits for them, and re-layouts  1.87 us (2%)
    pallas_call x1, Pallas kernels, shards(): pl.pallas_call(body, out_shape=jax.ShapeDtypeStruct((LEAVES, ROW), bf16),...  77.4 us
    unnamed x1, local copies, waits for them, and re-layouts  1.87 us

profile of v3, /device:TPU:0, one launch (start us, length us, event | category | flops | bytes accessed | tf_op | source)
XLA Modules:
  0.0 79.3 jit_solution(312657648465123200)
XLA Ops:
  0.0 77.4 %product.1 = bf16[512,512]{1,0:T(8,128)(2,1)} custom-call(bf16[64,64,512]{2,1,0:T(8,128)(2,1)} %bitcast.13, bf16[64,64,512]{2,1,0:T(8,128)(2,1)} %bitcast.14, bf16[2,64,64,512]{3,2,1,0:T(8,128)(2,1)} %bitcast.12, bf16[64,64,316]{2,1,0:T(8,128)(2,1)} %bitcast.15, bf16[64,64,316]{2,1,0:T(8,128)(2,1)} %bitcast.16, bf16[512,512]{1,0:T(8,128)(2,1)} %rhs_h.1, ...), custom_call_target="tpu_custom_call" | custom-call | tf_op jit(solution)/shard_map/product/pallas_call | solution.py:389
  77.4 1.9 %copy.15 = bf16[512,512]{1,0:T(8,128)(2,1)} copy(bf16[512,512]{1,0:T(8,128)(2,1)} %product.1) | data formatting | bytes 1048576
